TPU v7x, 256 devices: a whole 4x4x8 slice. The times are simulated.
256 devices in a mesh: slab: 8 (over x, y_lo), brick: 32 (over y_hi, z, core).
Axes of the slice: x: 4, y: 4 (y_hi: 2, y_lo: 2; y = y_hi * 2 + y_lo), z: 8, core: 2. Of those that a mesh axis runs over, the one named last changes fastest.
Arguments:
- positions: float32 [16384, 3, 128], P(('slab', 'brick')), may hold values from 0 to 9
- velocities: float32 [16384, 3, 128], P(('slab', 'brick')), may hold values from -6 to 6
- radius: float32 [16384, 128], P(('slab', 'brick')), may hold values from 0.35 to 0.65
- owners: int32 [16384], P(('slab', 'brick')), may hold values from 0 to 31, as said below
- neighbours: int32 [16384, 8], P(('slab', 'brick')), may hold values from 0 to 191, as said below
- cell_index: int32 [16384, 128], P(('slab', 'brick')), may hold values from 0 to 32767
Outputs:
- arrived: float32 [32768, 6, 128], P(('slab', 'brick'))
- field_grid: float32 [10, 64, 256, 512], P(None, 'slab', 'brick')
Inputs may be any that keep to these rules, and one draw needn't show every extreme that they name: `owners`: of the 64 blocks of one device, at most 4 name any one owner, and exactly 4 name some owner; in every slab one owner receives 4 blocks from every brick. `neighbours`: each row names 8 different places; never 64 plus the block's own place on its device; never a place below 64 on brick 0, nor one of 128 or more on the last brick.
All inputs are finite; a program needn't handle non-finite values.
Results may differ from a plain program's by a relative error of at most 0.00067.
Values sent between devices are 32-bit elements; how exact they have to be, the bound alone decides.
No kernel may reach another device: no remote copies, remote signals or barrier semaphores. Data moves between devices by JAX's collectives and lax.ppermute only.
A program may use at most 64 MiB of HBM per device.

v0:
```python
import math

import jax
import jax.numpy as jnp
from jax import lax
from jax.sharding import PartitionSpec as P

FIELDS = 10
RAD = 3
CZ = 8
CY = 8
CX = 512


STIFFNESS = 1.0
TIMESTEP = 0.1
FLOOR_SQ = 0.0625
GRAVITY = (0.5, 0.0, -0.866)
COMPONENT_PAIRS = ((0, 0), (1, 1), (2, 2), (0, 1), (0, 2), (1, 2))


def padded(block, sides, width):
    for axis, dim in sides:
        count = lax.axis_size(axis)
        forward = [(i, i + 1) for i in range(count - 1)]
        backward = [(target, source) for source, target in forward]
        low = lax.ppermute(
            lax.slice_in_dim(block, block.shape[dim] - width, None, axis=dim), axis, forward
        )
        high = lax.ppermute(lax.slice_in_dim(block, 0, width, axis=dim), axis, backward)
        block = jnp.concatenate([low, block, high], axis=dim)
    return block


def pair_terms(own_blocks, others):
    offset = own_blocks[:, None, :3, :, None] - others[:, :, :3, None, :]
    offset_sq = jnp.sum(offset * offset, axis=2)
    distance = jnp.sqrt(offset_sq + FLOOR_SQ)
    contact_reach = own_blocks[:, None, 3, :, None] + others[:, :, 3, None, :]
    intersection = jnp.maximum(contact_reach - distance, 0.0)
    push_scale = STIFFNESS * intersection / distance
    fabric_scale = intersection / (distance * distance)
    forces = jnp.sum(push_scale[:, :, None] * offset, axis=(1, 4))
    stress = jnp.stack(
        [
            jnp.sum(push_scale * offset[:, :, a] * offset[:, :, b], axis=(1, 3))
            for a, b in COMPONENT_PAIRS
        ],
        axis=1,
    )
    fabric = jnp.stack(
        [jnp.sum(fabric_scale * offset[:, :, a] * offset[:, :, a], axis=(1, 3)) for a in range(3)],
        axis=1,
    )
    return (forces, stress, fabric)


def contact_group(inputs_pair):
    return pair_terms(inputs_pair[0], inputs_pair[1])


def advance_state(positions, velocities, radius, forces, stress, fabric):
    masses = 8.0 * radius * radius * radius
    gravity = jnp.array(GRAVITY, dtype=jnp.float32)[None, :, None]
    new_velocity = velocities + TIMESTEP * (forces / masses[:, None, :] + gravity)
    new_position = positions + TIMESTEP * new_velocity
    fields = jnp.concatenate([stress, masses[:, None, :], fabric], axis=1)
    rounded = lax.optimization_barrier(fields.astype(jnp.bfloat16)).astype(jnp.float32)
    return jnp.concatenate([new_position, new_velocity, rounded], axis=1)


def kernel_weights():
    gauss_raw = [math.exp(-(t * t) / 4.5) for t in range(-RAD, RAD + 1)]
    norm_total = sum(gauss_raw)
    return [v / norm_total for v in gauss_raw]


def blur(field_data, axis_dim, extent):
    weights = kernel_weights()
    result = weights[0] * lax.slice_in_dim(field_data, 0, extent, axis=axis_dim)
    for t in range(1, 2 * RAD + 1):
        result = result + weights[t] * lax.slice_in_dim(field_data, t, t + extent, axis=axis_dim)
    return result


def deposit(field_values, cell_slots, slot_count):
    group_size = 8
    turns = slot_count // group_size
    block_width = field_values.shape[2]
    row_count = CZ * CY
    grouped_values = field_values.reshape(turns, group_size, FIELDS, block_width)
    grouped_cells = cell_slots.reshape(turns, group_size, block_width)

    def accumulate(running, inputs_pair):
        group_values, group_cells = inputs_pair
        across = (group_cells // CX)[None, :, :] == jnp.arange(row_count, dtype=jnp.int32)[
            :, None, None
        ]
        along = (
            (group_cells % CX)[:, :, None] == jnp.arange(CX, dtype=jnp.int32)[None, None, :]
        ).astype(jnp.bfloat16)
        weighted = jnp.where(
            across[None],
            jnp.transpose(group_values, (1, 0, 2))[:, None, :, :],
            jnp.zeros((), jnp.bfloat16),
        )
        running = running + jnp.einsum(
            "frgp,gpx->frx", weighted, along, preferred_element_type=jnp.float32
        )
        return (running, None)

    start_grid = jnp.zeros((FIELDS, row_count, CX), jnp.float32)
    tiles_grid, _ = lax.scan(accumulate, start_grid, (grouped_values, grouped_cells))
    return tiles_grid.reshape(FIELDS, CZ, CY, CX)


def body(positions, velocities, radius, owners, neighbours, cell_index):
    blocks_here = positions.shape[0]
    block_width = positions.shape[2]
    brick_count = lax.axis_size("brick")
    capacity = max(2, 2 * blocks_here // brick_count)
    slot_count = brick_count * capacity
    packed = jnp.concatenate([positions, radius[:, None, :]], axis=1)
    extended = padded(packed, (("brick", 0),), blocks_here)
    own_place = blocks_here + jnp.arange(blocks_here, dtype=jnp.int32)
    chosen = jnp.concatenate([own_place[:, None], neighbours], axis=1)
    others = extended[chosen]
    turns = blocks_here // 4
    partner_count = chosen.shape[1]
    forces, stress, fabric = lax.map(
        contact_group,
        (
            packed.reshape(turns, 4, 4, block_width),
            others.reshape(turns, 4, partner_count, 4, block_width),
        ),
    )
    forces = forces.reshape(blocks_here, 3, block_width)
    stress = stress.reshape(blocks_here, 6, block_width)
    fabric = fabric.reshape(blocks_here, 3, block_width)
    payload = advance_state(positions, velocities, radius, forces, stress, fabric)
    owner_hot = (owners[:, None] == jnp.arange(brick_count, dtype=jnp.int32)[None, :]).astype(
        jnp.int32
    )
    place_rank = jnp.sum((jnp.cumsum(owner_hot, axis=0) - owner_hot) * owner_hot, axis=1)
    slot_code = owners * capacity + place_rank
    matches = slot_code[None, :] == jnp.arange(slot_count, dtype=jnp.int32)[:, None]
    source_block = jnp.sum(
        jnp.where(matches, jnp.arange(blocks_here, dtype=jnp.int32)[None, :], 0), axis=1
    )
    filled = jnp.any(matches, axis=1)
    outgoing = jnp.where(filled[:, None, None], payload[source_block], 0.0).reshape(
        brick_count, capacity, 16, block_width
    )
    out_cells = jnp.where(filled[:, None], cell_index[source_block], 0).reshape(
        brick_count, capacity, block_width
    )
    moved, moved_cells = (
        lax.all_to_all(outgoing, "brick", split_axis=0, concat_axis=0, tiled=True),
        lax.all_to_all(out_cells, "brick", split_axis=0, concat_axis=0, tiled=True),
    )
    moved = moved.reshape(slot_count, 16, block_width)
    moved_cells = moved_cells.reshape(slot_count, block_width)
    arrived = moved[:, :6]
    field_values = moved[:, 6:].astype(jnp.bfloat16)
    tiles_grid = deposit(field_values, moved_cells, slot_count)
    smooth_x = blur(jnp.pad(tiles_grid, ((0, 0), (0, 0), (0, 0), (RAD, RAD))), 3, CX)
    beside_rows = padded(smooth_x, (("brick", 2),), RAD)
    smooth_y = blur(beside_rows, 2, CY)
    beside_layers = padded(smooth_y, (("slab", 1),), RAD)
    field_grid = blur(beside_layers, 1, CZ)
    return (arrived, field_grid)


def solution(mesh):
    return jax.shard_map(
        body,
        mesh=mesh,
        in_specs=(
            P(("slab", "brick"), None, None),
            P(("slab", "brick"), None, None),
            P(("slab", "brick"), None),
            P(("slab", "brick")),
            P(("slab", "brick"), None),
            P(("slab", "brick"), None),
        ),
        out_specs=(P(("slab", "brick"), None, None), P(None, "slab", "brick", None)),
        check_vma=False,
    )
```

profile of v0, /device:TPU:37, one launch (start us, length us, event | category | flops | bytes accessed | tf_op | source)
XLA Modules:
  0.0 265.9 jit_solution(12031489054779362191)
XLA Ops:
  2.4 4.1 %collective-permute-start = (f32[64,4,128]{2,1,0:T(4,128)S(1)}, f32[64,4,128]{2,1,0:T(4,128)S(1)}, u32[]{:S(2)}, u32[]{:S(2)}) collective-permute-start(f32[64,4,128]{2,1,0:T(4,128)S(1)} %pad_maximum_fusion.8), channel_id=1, source_target_pairs={{0,1},{1,2},{2,3},{3,4},{4,5},{5,6},{6,7},{7,8},{8,9},{9,10},{10,1... | collective-permute-start | bytes 393224 | tf_op jit(solution)/shard_map/ppermute | solution.py:27
  6.6 1.9 collective-permute-start.1
  14.7 2.7 %gather_fusion = f32[576,4,128]{2,1,0:T(4,128)S(1)} fusion(f32[192,4,128]{2,1,0:T(4,128)S(1)} %pad_maximum_fusion.5, s32[1024]{0:T(1024)S(1)} %pad_clamp_fusion.1), kind=kCustom, calls=%fused_computation | custom fusion | bytes 2361600 | tf_op jit(solution)/shard_map/gather | solution.py:127
  17.4 122.4 %while.27 = (s32[]{:T(128)}, f32[16,4,3,128]{3,1,0,2:T(4,128)S(1)}, bf16[16,4,6,128]{3,1,2,0:T(4,128)(2,1)S(1)}, bf16[16,4,3,128]{3,1,2,0:T(4,128)(2,1)S(1)}, f3...) while((s32[]{:T(128)}, f32[16,4,3,128]{3,1,0,2:T(4,128)S(1)}, ...), condition=%wide.region_15.16_spmd, body=%wide.region_3.15_spmd.sunk | while | flops 28314624 | bytes 24196192 | solution.py:130
  17.5 1.4 multiply_reduce_fusion.9
  19.0 4.9 %fusion.82 = (bf16[4,128]{1,0:T(4,128)(2,1)S(1)}, bf16[4,128]{1,0:T(4,128)(2,1)S(1)}, bf16[4,128]{1,0:T(4,128)(2,1)S(1)}, bf16[4,128]{1,0:T(4,128)(2,1)S(1)}, bf...) fusion(f32[4,9,3,128,128]{4,3,1,0,2:T(8,128)S(1)} %get-tuple-el, ...), kind=kLoop, calls=%fused_computation.11.clone.1 | loop fusion | flops 18279936 | bytes 11826176 | tf_op jit(solution)/shard_map/while/body/eval_jaxpr/reduce_sum | solution.py:52
  25.2 1.4 multiply_reduce_fusion.9
  26.7 4.9 %fusion.82 = (bf16[4,128]{1,0:T(4,128)(2,1)S(1)}, bf16[4,128]{1,0:T(4,128)(2,1)S(1)}, bf16[4,128]{1,0:T(4,128)(2,1)S(1)}, bf16[4,128]{1,0:T(4,128)(2,1)S(1)}, bf...) fusion(f32[4,9,3,128,128]{4,3,1,0,2:T(8,128)S(1)} %get-tuple-el, ...), kind=kLoop, calls=%fused_computation.11.clone.1 | loop fusion | flops 18279936 | bytes 11826176 | tf_op jit(solution)/shard_map/while/body/eval_jaxpr/reduce_sum | solution.py:52
  32.8 1.4 multiply_reduce_fusion.9
  34.3 4.9 %fusion.82 = (bf16[4,128]{1,0:T(4,128)(2,1)S(1)}, bf16[4,128]{1,0:T(4,128)(2,1)S(1)}, bf16[4,128]{1,0:T(4,128)(2,1)S(1)}, bf16[4,128]{1,0:T(4,128)(2,1)S(1)}, bf...) fusion(f32[4,9,3,128,128]{4,3,1,0,2:T(8,128)S(1)} %get-tuple-el, ...), kind=kLoop, calls=%fused_computation.11.clone.1 | loop fusion | flops 18279936 | bytes 11826176 | tf_op jit(solution)/shard_map/while/body/eval_jaxpr/reduce_sum | solution.py:52
  40.5 1.4 multiply_reduce_fusion.9
  42.0 4.9 %fusion.82 = (bf16[4,128]{1,0:T(4,128)(2,1)S(1)}, bf16[4,128]{1,0:T(4,128)(2,1)S(1)}, bf16[4,128]{1,0:T(4,128)(2,1)S(1)}, bf16[4,128]{1,0:T(4,128)(2,1)S(1)}, bf...) fusion(f32[4,9,3,128,128]{4,3,1,0,2:T(8,128)S(1)} %get-tuple-el, ...), kind=kLoop, calls=%fused_computation.11.clone.1 | loop fusion | flops 18279936 | bytes 11826176 | tf_op jit(solution)/shard_map/while/body/eval_jaxpr/reduce_sum | solution.py:52
  48.1 1.4 multiply_reduce_fusion.9
  49.6 4.9 %fusion.82 = (bf16[4,128]{1,0:T(4,128)(2,1)S(1)}, bf16[4,128]{1,0:T(4,128)(2,1)S(1)}, bf16[4,128]{1,0:T(4,128)(2,1)S(1)}, bf16[4,128]{1,0:T(4,128)(2,1)S(1)}, bf...) fusion(f32[4,9,3,128,128]{4,3,1,0,2:T(8,128)S(1)} %get-tuple-el, ...), kind=kLoop, calls=%fused_computation.11.clone.1 | loop fusion | flops 18279936 | bytes 11826176 | tf_op jit(solution)/shard_map/while/body/eval_jaxpr/reduce_sum | solution.py:52
  55.8 1.4 multiply_reduce_fusion.9
  57.3 4.9 %fusion.82 = (bf16[4,128]{1,0:T(4,128)(2,1)S(1)}, bf16[4,128]{1,0:T(4,128)(2,1)S(1)}, bf16[4,128]{1,0:T(4,128)(2,1)S(1)}, bf16[4,128]{1,0:T(4,128)(2,1)S(1)}, bf...) fusion(f32[4,9,3,128,128]{4,3,1,0,2:T(8,128)S(1)} %get-tuple-el, ...), kind=kLoop, calls=%fused_computation.11.clone.1 | loop fusion | flops 18279936 | bytes 11826176 | tf_op jit(solution)/shard_map/while/body/eval_jaxpr/reduce_sum | solution.py:52
  63.4 1.4 multiply_reduce_fusion.9
  64.9 4.9 %fusion.82 = (bf16[4,128]{1,0:T(4,128)(2,1)S(1)}, bf16[4,128]{1,0:T(4,128)(2,1)S(1)}, bf16[4,128]{1,0:T(4,128)(2,1)S(1)}, bf16[4,128]{1,0:T(4,128)(2,1)S(1)}, bf...) fusion(f32[4,9,3,128,128]{4,3,1,0,2:T(8,128)S(1)} %get-tuple-el, ...), kind=kLoop, calls=%fused_computation.11.clone.1 | loop fusion | flops 18279936 | bytes 11826176 | tf_op jit(solution)/shard_map/while/body/eval_jaxpr/reduce_sum | solution.py:52
  71.1 1.4 multiply_reduce_fusion.9
  72.6 4.9 %fusion.82 = (bf16[4,128]{1,0:T(4,128)(2,1)S(1)}, bf16[4,128]{1,0:T(4,128)(2,1)S(1)}, bf16[4,128]{1,0:T(4,128)(2,1)S(1)}, bf16[4,128]{1,0:T(4,128)(2,1)S(1)}, bf...) fusion(f32[4,9,3,128,128]{4,3,1,0,2:T(8,128)S(1)} %get-tuple-el, ...), kind=kLoop, calls=%fused_computation.11.clone.1 | loop fusion | flops 18279936 | bytes 11826176 | tf_op jit(solution)/shard_map/while/body/eval_jaxpr/reduce_sum | solution.py:52
  78.7 1.4 multiply_reduce_fusion.9
  80.2 4.9 %fusion.82 = (bf16[4,128]{1,0:T(4,128)(2,1)S(1)}, bf16[4,128]{1,0:T(4,128)(2,1)S(1)}, bf16[4,128]{1,0:T(4,128)(2,1)S(1)}, bf16[4,128]{1,0:T(4,128)(2,1)S(1)}, bf...) fusion(f32[4,9,3,128,128]{4,3,1,0,2:T(8,128)S(1)} %get-tuple-el, ...), kind=kLoop, calls=%fused_computation.11.clone.1 | loop fusion | flops 18279936 | bytes 11826176 | tf_op jit(solution)/shard_map/while/body/eval_jaxpr/reduce_sum | solution.py:52
  86.4 1.4 multiply_reduce_fusion.9
  87.9 4.9 %fusion.82 = (bf16[4,128]{1,0:T(4,128)(2,1)S(1)}, bf16[4,128]{1,0:T(4,128)(2,1)S(1)}, bf16[4,128]{1,0:T(4,128)(2,1)S(1)}, bf16[4,128]{1,0:T(4,128)(2,1)S(1)}, bf...) fusion(f32[4,9,3,128,128]{4,3,1,0,2:T(8,128)S(1)} %get-tuple-el, ...), kind=kLoop, calls=%fused_computation.11.clone.1 | loop fusion | flops 18279936 | bytes 11826176 | tf_op jit(solution)/shard_map/while/body/eval_jaxpr/reduce_sum | solution.py:52
  94.0 1.4 multiply_reduce_fusion.9
  95.5 4.9 %fusion.82 = (bf16[4,128]{1,0:T(4,128)(2,1)S(1)}, bf16[4,128]{1,0:T(4,128)(2,1)S(1)}, bf16[4,128]{1,0:T(4,128)(2,1)S(1)}, bf16[4,128]{1,0:T(4,128)(2,1)S(1)}, bf...) fusion(f32[4,9,3,128,128]{4,3,1,0,2:T(8,128)S(1)} %get-tuple-el, ...), kind=kLoop, calls=%fused_computation.11.clone.1 | loop fusion | flops 18279936 | bytes 11826176 | tf_op jit(solution)/shard_map/while/body/eval_jaxpr/reduce_sum | solution.py:52
  101.7 1.4 multiply_reduce_fusion.9
  103.2 4.9 %fusion.82 = (bf16[4,128]{1,0:T(4,128)(2,1)S(1)}, bf16[4,128]{1,0:T(4,128)(2,1)S(1)}, bf16[4,128]{1,0:T(4,128)(2,1)S(1)}, bf16[4,128]{1,0:T(4,128)(2,1)S(1)}, bf...) fusion(f32[4,9,3,128,128]{4,3,1,0,2:T(8,128)S(1)} %get-tuple-el, ...), kind=kLoop, calls=%fused_computation.11.clone.1 | loop fusion | flops 18279936 | bytes 11826176 | tf_op jit(solution)/shard_map/while/body/eval_jaxpr/reduce_sum | solution.py:52
  109.3 1.4 multiply_reduce_fusion.9
  110.8 4.9 %fusion.82 = (bf16[4,128]{1,0:T(4,128)(2,1)S(1)}, bf16[4,128]{1,0:T(4,128)(2,1)S(1)}, bf16[4,128]{1,0:T(4,128)(2,1)S(1)}, bf16[4,128]{1,0:T(4,128)(2,1)S(1)}, bf...) fusion(f32[4,9,3,128,128]{4,3,1,0,2:T(8,128)S(1)} %get-tuple-el, ...), kind=kLoop, calls=%fused_computation.11.clone.1 | loop fusion | flops 18279936 | bytes 11826176 | tf_op jit(solution)/shard_map/while/body/eval_jaxpr/reduce_sum | solution.py:52
  117.0 1.4 multiply_reduce_fusion.9
  118.5 4.9 %fusion.82 = (bf16[4,128]{1,0:T(4,128)(2,1)S(1)}, bf16[4,128]{1,0:T(4,128)(2,1)S(1)}, bf16[4,128]{1,0:T(4,128)(2,1)S(1)}, bf16[4,128]{1,0:T(4,128)(2,1)S(1)}, bf...) fusion(f32[4,9,3,128,128]{4,3,1,0,2:T(8,128)S(1)} %get-tuple-el, ...), kind=kLoop, calls=%fused_computation.11.clone.1 | loop fusion | flops 18279936 | bytes 11826176 | tf_op jit(solution)/shard_map/while/body/eval_jaxpr/reduce_sum | solution.py:52
  124.6 1.4 multiply_reduce_fusion.9
  126.1 4.9 %fusion.82 = (bf16[4,128]{1,0:T(4,128)(2,1)S(1)}, bf16[4,128]{1,0:T(4,128)(2,1)S(1)}, bf16[4,128]{1,0:T(4,128)(2,1)S(1)}, bf16[4,128]{1,0:T(4,128)(2,1)S(1)}, bf...) fusion(f32[4,9,3,128,128]{4,3,1,0,2:T(8,128)S(1)} %get-tuple-el, ...), kind=kLoop, calls=%fused_computation.11.clone.1 | loop fusion | flops 18279936 | bytes 11826176 | tf_op jit(solution)/shard_map/while/body/eval_jaxpr/reduce_sum | solution.py:52
  132.3 1.4 multiply_reduce_fusion.9
  133.8 4.9 %fusion.82 = (bf16[4,128]{1,0:T(4,128)(2,1)S(1)}, bf16[4,128]{1,0:T(4,128)(2,1)S(1)}, bf16[4,128]{1,0:T(4,128)(2,1)S(1)}, bf16[4,128]{1,0:T(4,128)(2,1)S(1)}, bf...) fusion(f32[4,9,3,128,128]{4,3,1,0,2:T(8,128)S(1)} %get-tuple-el, ...), kind=kLoop, calls=%fused_computation.11.clone.1 | loop fusion | flops 18279936 | bytes 11826176 | tf_op jit(solution)/shard_map/while/body/eval_jaxpr/reduce_sum | solution.py:52
  142.2 1.4 copy.172
  143.5 12.4 %all-to-all-start = ((f32[32,4,16,128]{3,1,2,0:T(4,128)}), f32[32,4,16,128]{3,1,2,0:T(4,128)S(1)}, u32[]{:S(2)}, u32[]{:S(2)}) async-start(f32[32,4,16,128]{3,1,2,0:T(4,128)} %copy.172), calls=%async_computation | async-start | bytes 2097152 | tf_op jit(solution)/shard_map/all_to_all | solution.py:158
  157.4 28.1 %all-to-all-done = f32[32,4,16,128]{3,1,2,0:T(4,128)S(1)} async-done(((f32[32,4,16,128]{3,1,2,0:T(4,128)}), f32[32,4,16,128]{3,1,2,0:T(4,128)S(1)}, u32[]{:S(2)}, u32[]{:S(2)}) %all-to-all-start) | async-done | bytes 1048608 | tf_op jit(solution)/shard_map/all_to_all | solution.py:158
  185.4 4.5 %all-to-all-start.1 = ((s32[32,4,128]{2,1,0:T(4,128)}), s32[32,4,128]{2,1,0:T(4,128)S(1)}, u32[]{:S(2)}, u32[]{:S(2)}) async-start(s32[32,4,128]{2,1,0:T(4,128)} %broadcast_select_fusion.1), calls=%async_computation.1 | async-start | bytes 131072 | tf_op jit(solution)/shard_map/all_to_all | solution.py:159
  190.3 8.4 %all-to-all-done.1 = s32[32,4,128]{2,1,0:T(4,128)S(1)} async-done(((s32[32,4,128]{2,1,0:T(4,128)}), s32[32,4,128]{2,1,0:T(4,128)S(1)}, u32[]{:S(2)}, u32[]{:S(2)}) %all-to-all-start.1) | async-done | bytes 65568 | tf_op jit(solution)/shard_map/all_to_all | solution.py:159
  198.7 20.5 %while.28 = (s32[]{:T(128)}, f32[10,64,512]{2,1,0:T(8,128)S(1)}, s32[16,8,128]{2,1,0:T(8,128)S(1)}, bf16[16,8,10,128]{3,1,2,0:T(8,128)(2,1)S(1)}, s32[]{:T(128)}, /*index=5*/s32[]{:T(128)}) while((s32[]{:T(128)}, f32[10,64,512]{2,1,0:T(8,128)S(1)}, s32[16,8,128]{2,1,0:T(8,128)S(1)}, bf16[16,8,10,128]{3,1,2,0:T(8,128)(2,1)S(1)}, ...), condition=%wide.region_18.19_spmd.clone, body=%wide.region_17.18_spmd.clone.sunk | while | flops 673015808 | bytes 2838619 | solution.py:113
  202.6 1.1 fusion.87
  203.9 1.1 fusion.87
  205.2 1.1 fusion.87
  206.5 1.1 fusion.87
  207.7 1.1 fusion.87
  209.0 1.1 fusion.87
  210.3 1.1 fusion.87
  211.6 1.1 fusion.87
  212.9 1.1 fusion.87
  214.1 1.1 fusion.87
  215.4 1.1 fusion.87
  219.1 2.1 fusion.46
  221.7 3.0 %collective-permute-start.2 = (f32[10,8,3,512]{3,1,2,0:T(8,128)S(1)}, f32[10,8,3,512]{3,1,2,0:T(8,128)S(1)}, u32[]{:S(2)}, u32[]{:S(2)}) collective-permute-start(f32[10,8,3,512]{3,1,2,0:T(8,128)S(1)} %copy.175), channel_id=1, source_target_pairs={{0,1},{1,2},{2,3},{3,4},{4,5},{5,6},{6,7},{7,8},{8,9},{9,10},{10,1... | collective-permute-start | bytes 1474568 | tf_op jit(solution)/shard_map/ppermute | solution.py:27
  224.8 1.9 collective-permute-start.3
  226.8 3.7 %collective-permute-done.2 = f32[10,8,3,512]{3,1,2,0:T(8,128)S(1)} collective-permute-done((f32[10,8,3,512]{3,1,2,0:T(8,128)S(1)}, f32[10,8,3,512]{3,1,2,0:T(8,128)S(1)}, u32[]{:S(2)}, u32[]{:S(2)}) %collective-permute-start.2) | collective-permute-done | bytes 491552 | tf_op jit(solution)/shard_map/ppermute | solution.py:27
  230.8 4.2 %collective-permute-done.3 = f32[10,8,3,512]{3,1,2,0:T(8,128)S(1)} collective-permute-done((f32[10,8,3,512]{3,1,2,0:T(8,128)S(1)}, f32[10,8,3,512]{3,1,2,0:T(8,128)S(1)}, u32[]{:S(2)}, u32[]{:S(2)}) %collective-permute-start.3) | collective-permute-done | bytes 491552 | tf_op jit(solution)/shard_map/ppermute | solution.py:30
  235.3 1.9 fusion.55
  237.3 2.3 collective-permute-start.4
  239.7 3.9 %collective-permute-start.5 = (f32[10,3,8,512]{3,2,1,0:T(8,128)S(1)}, f32[10,3,8,512]{3,2,1,0:T(8,128)S(1)}, u32[]{:S(2)}, u32[]{:S(2)}) collective-permute-start(f32[10,3,8,512]{3,2,1,0:T(8,128)S(1)} %get-tuple-element.202), channel_id=1, source_target_pairs={{32,0},{64,32},{96,64},{128,96},{160,128},{192,160},{224,192},{33,... | collective-permute-start | bytes 1474568 | tf_op jit(solution)/shard_map/ppermute | solution.py:30
  244.4 16.5 %collective-permute-done.4 = f32[10,3,8,512]{3,2,1,0:T(8,128)S(1)} collective-permute-done((f32[10,3,8,512]{3,2,1,0:T(8,128)S(1)}, f32[10,3,8,512]{3,2,1,0:T(8,128)S(1)}, u32[]{:S(2)}, u32[]{:S(2)}) %collective-permute-start.4) | collective-permute-done | bytes 491552 | tf_op jit(solution)/shard_map/ppermute | solution.py:27
  260.9 2.9 %collective-permute-done.5 = f32[10,3,8,512]{3,2,1,0:T(8,128)S(1)} collective-permute-done((f32[10,3,8,512]{3,2,1,0:T(8,128)S(1)}, f32[10,3,8,512]{3,2,1,0:T(8,128)S(1)}, u32[]{:S(2)}, u32[]{:S(2)}) %collective-permute-start.5) | collective-permute-done | bytes 491552 | tf_op jit(solution)/shard_map/ppermute | solution.py:30
  263.9 2.0 fusion.29
  (416 shorter events, 39.3 us)
Async XLA Ops:
  0.6 155.3 %copy-start = (s32[64,128]{1,0:T(8,128)S(1)}, s32[64,128]{1,0:T(8,128)}, u32[]{:S(2)}) copy-start(s32[64,128]{1,0:T(8,128)} %param.16) | copy-start | bytes 98308
  2.4 11.3 %collective-permute-start = (f32[64,4,128]{2,1,0:T(4,128)S(1)}, f32[64,4,128]{2,1,0:T(4,128)S(1)}, u32[]{:S(2)}, u32[]{:S(2)}) collective-permute-start(f32[64,4,128]{2,1,0:T(4,128)S(1)} %pad_maximum_fusion.8), channel_id=1, source_target_pairs={{0,1},{1,2},{2,3},{3,4},{4,5},{5,6},{6,7},{7,8},{8,9},{9,10},{10,1... | collective-permute-start | bytes 393224 | tf_op jit(solution)/shard_map/ppermute | solution.py:27
  6.6 7.2 %collective-permute-start.1 = (f32[64,4,128]{2,1,0:T(4,128)S(1)}, f32[64,4,128]{2,1,0:T(4,128)S(1)}, u32[]{:S(2)}, u32[]{:S(2)}) collective-permute-start(f32[64,4,128]{2,1,0:T(4,128)S(1)} %pad_maximum_fusion.8), channel_id=1, source_target_pairs={{1,0},{2,1},{3,2},{4,3},{5,4},{6,5},{7,6},{8,7},{9,8},{10,9},{11,1... | collective-permute-start | bytes 393224 | tf_op jit(solution)/shard_map/ppermute | solution.py:30
  139.9 0.9 copy-start.1
  139.9 0.9 copy-start.2
  139.9 0.9 copy-start.3
  143.5 41.9 %all-to-all-start = ((f32[32,4,16,128]{3,1,2,0:T(4,128)}), f32[32,4,16,128]{3,1,2,0:T(4,128)S(1)}, u32[]{:S(2)}, u32[]{:S(2)}) async-start(f32[32,4,16,128]{3,1,2,0:T(4,128)} %copy.172), calls=%async_computation | async-start | bytes 2097152 | tf_op jit(solution)/shard_map/all_to_all | solution.py:158
  185.4 13.2 %all-to-all-start.1 = ((s32[32,4,128]{2,1,0:T(4,128)}), s32[32,4,128]{2,1,0:T(4,128)S(1)}, u32[]{:S(2)}, u32[]{:S(2)}) async-start(s32[32,4,128]{2,1,0:T(4,128)} %broadcast_select_fusion.1), calls=%async_computation.1 | async-start | bytes 131072 | tf_op jit(solution)/shard_map/all_to_all | solution.py:159
  221.7 8.8 %collective-permute-start.2 = (f32[10,8,3,512]{3,1,2,0:T(8,128)S(1)}, f32[10,8,3,512]{3,1,2,0:T(8,128)S(1)}, u32[]{:S(2)}, u32[]{:S(2)}) collective-permute-start(f32[10,8,3,512]{3,1,2,0:T(8,128)S(1)} %copy.175), channel_id=1, source_target_pairs={{0,1},{1,2},{2,3},{3,4},{4,5},{5,6},{6,7},{7,8},{8,9},{9,10},{10,1... | collective-permute-start | bytes 1474568 | tf_op jit(solution)/shard_map/ppermute | solution.py:27
  224.8 10.1 %collective-permute-start.3 = (f32[10,8,3,512]{3,1,2,0:T(8,128)S(1)}, f32[10,8,3,512]{3,1,2,0:T(8,128)S(1)}, u32[]{:S(2)}, u32[]{:S(2)}) collective-permute-start(f32[10,8,3,512]{3,1,2,0:T(8,128)S(1)} %copy.177), channel_id=1, source_target_pairs={{1,0},{2,1},{3,2},{4,3},{5,4},{6,5},{7,6},{8,7},{9,8},{10,9},{11,1... | collective-permute-start | bytes 1474568 | tf_op jit(solution)/shard_map/ppermute | solution.py:30
  237.3 23.6 %collective-permute-start.4 = (f32[10,3,8,512]{3,2,1,0:T(8,128)S(1)}, f32[10,3,8,512]{3,2,1,0:T(8,128)S(1)}, u32[]{:S(2)}, u32[]{:S(2)}) collective-permute-start(f32[10,3,8,512]{3,2,1,0:T(8,128)S(1)} %get-tuple-element.201), channel_id=1, source_target_pairs={{0,32},{32,64},{64,96},{96,128},{128,160},{160,192},{192,224},{1,3... | collective-permute-start | bytes 1474568 | tf_op jit(solution)/shard_map/ppermute | solution.py:27
  239.7 24.2 %collective-permute-start.5 = (f32[10,3,8,512]{3,2,1,0:T(8,128)S(1)}, f32[10,3,8,512]{3,2,1,0:T(8,128)S(1)}, u32[]{:S(2)}, u32[]{:S(2)}) collective-permute-start(f32[10,3,8,512]{3,2,1,0:T(8,128)S(1)} %get-tuple-element.202), channel_id=1, source_target_pairs={{32,0},{64,32},{96,64},{128,96},{160,128},{192,160},{224,192},{33,... | collective-permute-start | bytes 1474568 | tf_op jit(solution)/shard_map/ppermute | solution.py:30
where the time goes:
time: 267 us; the launch traced here: 266 us
  other arithmetic  133 us (50%)
  waiting for transfers between devices  63.8 us (24%)
  starting transfers between devices  34.1 us (13%)
  matrix products  18.3 us (7%)
  local copies, waits for them, and re-layouts  12.8 us (5%)
  loops' own time  2.94 us (1%)
    reduce_sum x16, other arithmetic, pair_terms(): jnp.sum(fabric_scale * offset[:, :, a] * offset[:, :, a], axis=(1, 3))  79.1 us
    all_to_all x1, waiting for transfers between devices, body(): lax.all_to_all(outgoing, 'brick', split_axis=0, concat_axis=0, tiled=True)  28.1 us
    reduce_sum x16, other arithmetic, pair_terms(): offset_sq = jnp.sum(offset * offset, axis=2)  22.9 us
    ppermute x3, waiting for transfers between devices, padded(): lax.ppermute(lax.slice_in_dim(block, block.shape[dim] - width, None, axis...  20.2 us
    dot_general x16, matrix products, accumulate(): jnp.einsum('frgp,gpx->frx', weighted, along, preferred_element_type=jnp.f...  18.3 us
    reduce_sum x16, other arithmetic, pair_terms(): forces = jnp.sum(push_scale[:, :, None] * offset, axis=(1, 4))  15.6 us
    all_to_all x1, starting transfers between devices, body(): lax.all_to_all(outgoing, 'brick', split_axis=0, concat_axis=0, tiled=True)  12.4 us
    ppermute x3, starting transfers between devices, padded(): lax.ppermute(lax.slice_in_dim(block, block.shape[dim] - width, None, axis...  9.43 us
  transfers between devices with their start and end apart: 8, of which 6 were waited for; matrix products, arithmetic and copies ran while one was open for 3% of the time, Pallas kernels for 0%

commit v1 on v0

v1 whole, which is shorter than its diff:
```python
import math

import jax
import jax.numpy as jnp
from jax import lax
from jax.experimental import pallas as pl
from jax.experimental.pallas import tpu as pltpu
from jax.sharding import PartitionSpec as P

FIELDS = 10
RAD = 3
CZ = 8
CY = 8
CX = 512
CAP = 4
NB = 64
PB = 128
K = 8
BRICKS = 32
SLABS = 8
EARLY = 6
LATE = 12
FEAT = 32

TIMESTEP = 0.1
FLOOR_SQ = 0.0625
GRAVITY = (0.5, 0.0, -0.866)
PAIRS = ((0, 0), (1, 1), (2, 2), (0, 1), (0, 2), (1, 2))
CENTRE = 4.5
BF16 = jnp.bfloat16
F32 = jnp.float32


def kernel_weights():
    raw = [math.exp(-(t * t) / 4.5) for t in range(-RAD, RAD + 1)]
    total = sum(raw)
    return [v / total for v in raw]


def split3(value):
    high = value.astype(BF16).astype(F32)
    rest = value - high
    mid = rest.astype(BF16).astype(F32)
    return high, mid, rest - mid


def vmem():
    return pl.BlockSpec(memory_space=pltpu.VMEM)


def smem():
    return pl.BlockSpec(memory_space=pltpu.SMEM)


def clear_counts(counts):
    def clear(o, carry):
        counts[o] = 0
        return carry

    lax.fori_loop(0, BRICKS, clear, 0)


def next_slot(owners, counts, i):
    owner = owners[i]
    rank = counts[owner]
    counts[owner] = rank + 1
    return owner, rank


def early_kernel(owners, place, radius, cells, out, counts):
    clear_counts(counts)
    out[...] = jnp.zeros_like(out)

    def place_block(i, carry):
        owner, rank = next_slot(owners, counts, i)
        row = owner * (CAP * EARLY) + rank * EARLY
        for a in range(3):
            out[pl.ds(row + a, 1), :] = place[a, pl.ds(i, 1), :]
        out[pl.ds(row + 3, 1), :] = radius[pl.ds(i, 1), :]
        out[pl.ds(row + 4, 1), :] = cells[pl.ds(i, 1), :].astype(F32)
        return carry

    lax.fori_loop(0, NB, place_block, 0)


def early_payload(owners, place, radius, cells):
    return pl.pallas_call(
        early_kernel,
        out_shape=jax.ShapeDtypeStruct((BRICKS * CAP * EARLY, PB), F32),
        in_specs=[smem(), vmem(), vmem(), vmem()],
        out_specs=vmem(),
        scratch_shapes=[pltpu.SMEM((BRICKS,), jnp.int32)],
        name="early_payload",
    )(owners, place, radius, cells)


def contact_kernel(
    neighbours, owners, low, own, high, velocity, out, lane_masks, feat_rows, feat, own_feat, moment_rows, moments, sums, late, counts
):
    lane_group = lax.broadcasted_iota(jnp.int32, (PB, PB), 1) // FEAT
    for j in range(4):
        lane_masks[j] = jnp.where(lane_group == j, 1.0, 0.0).astype(BF16)
    for part, source in enumerate((low, own, high)):
        centred = [source[a] - CENTRE for a in range(3)]
        splits = [split3(c) for c in centred]
        norm = split3(centred[0] * centred[0] + centred[1] * centred[1] + centred[2] * centred[2])
        reach = split3(source[3])
        one = jnp.ones((NB, PB), F32)
        zero = jnp.zeros((NB, PB), F32)
        rows = []
        for h, m, l in splits:
            rows += [h, h, h, m, m, l]
        rows += [one] * 3 + list(norm) + list(reach)
        rows += [zero] * (FEAT - len(rows))
        for k, row in enumerate(rows):
            feat_rows[pl.ds(k, NB, stride=FEAT), :] = row

        for g in range(NB // 4):
            feat[part * (NB // 4) + g] = feat_rows[g * 128 : (g + 1) * 128, :].T.astype(BF16)
        x, y, z = centred
        basis = [x, y, z, x * x, y * y, z * z, x * y, x * z, y * z]
        parts = [split3(v) for v in basis]
        rows = [one] + [p[0] for p in parts] + [p[1] for p in parts] + [p[2] for p in parts]
        rows += [zero] * (FEAT - len(rows))
        for k, row in enumerate(rows):
            moment_rows[pl.ds(k, NB, stride=FEAT), :] = row
        for g in range(4):
            moments[pl.ds(part * NB + g * 16, 16)] = (
                moment_rows[g * 16 * FEAT : (g + 1) * 16 * FEAT, :].reshape(16, FEAT, PB).astype(BF16)
            )
        if part == 1:
            rows = []
            for h, m, l in splits:
                rows += [-2.0 * h, -2.0 * m, -2.0 * l, -2.0 * h, -2.0 * m, -2.0 * h]
            floored = split3(
                centred[0] * centred[0] + centred[1] * centred[1] + centred[2] * centred[2] + FLOOR_SQ
            )
            rows += list(floored) + [one] * 3
            rows += [zero] * (FEAT - len(rows))
            reach_rows = [zero] * 18 + list(reach) + [zero] * 3 + [one] * 3
            reach_rows += [zero] * (FEAT - len(reach_rows))
            for half, half_rows in enumerate((rows, reach_rows)):
                for k, row in enumerate(half_rows):
                    feat_rows[pl.ds(k, NB, stride=FEAT), :] = row
                for g in range(4):
                    own_feat[pl.ds(g * 16, 16), :, half * PB : (half + 1) * PB] = (
                        feat_rows[g * 16 * FEAT : (g + 1) * 16 * FEAT, :].reshape(16, FEAT, PB).astype(BF16)
                    )

    def block(i, carry):
        places = [NB + i] + [neighbours[i, k] for k in range(K)]
        weights = jnp.concatenate([own_feat[i]] * 4, axis=0)
        total = None
        for g in range(0, K + 1, 3):
            others = jnp.concatenate([feat[e >> 2] * lane_masks[e & 3] for e in places[g : g + 3]], axis=0)
            pair = jnp.dot(others, weights, preferred_element_type=F32)
            inverse = lax.rsqrt(pair[:, :PB])
            push = jnp.maximum(pair[:, PB:] * inverse - 1.0, 0.0)
            bend = push * inverse
            scales = jnp.concatenate([push.astype(BF16), bend.astype(BF16)], axis=1)
            basis = jnp.concatenate([moments[e] for e in places[g : g + 3]], axis=1)
            part = jnp.dot(basis, scales, preferred_element_type=F32)
            total = part if total is None else total + part
        sums[i] = total
        return carry

    lax.fori_loop(0, NB, block, 0, unroll=4)

    def summed(k, half):
        lanes = slice(half * PB, (half + 1) * PB)
        value = sums[:, k, lanes]
        if k:
            value = value + sums[:, k + 9, lanes] + sums[:, k + 18, lanes]
        return value

    centred = [own[a] - CENTRE for a in range(3)]
    weight = summed(0, 0)
    first = [summed(1 + a, 0) for a in range(3)]
    forces = [centred[a] * weight - first[a] for a in range(3)]
    results = []
    mass = 8.0 * own[3] * own[3] * own[3]
    for a in range(3):
        results.append(velocity[a] + TIMESTEP * (forces[a] / mass + GRAVITY[a]))
    for n, (a, b) in enumerate(PAIRS):
        results.append(
            (centred[a] * centred[b]) * weight - centred[a] * first[b] - centred[b] * first[a] + summed(4 + n, 0)
        )
    bent = summed(0, 1)
    for a in range(3):
        results.append(
            (centred[a] * centred[a]) * bent - 2.0 * (centred[a] * summed(1 + a, 1)) + summed(4 + a, 1)
        )
    for f, value in enumerate(results):
        late[f] = value

    clear_counts(counts)
    out[...] = jnp.zeros_like(out)

    def place_block(i, carry):
        owner, rank = next_slot(owners, counts, i)
        row = owner * (CAP * LATE) + rank * LATE
        for f in range(LATE):
            out[pl.ds(row + f, 1), :] = late[f, pl.ds(i, 1), :]
        return carry

    lax.fori_loop(0, NB, place_block, 0)


def contact_payload(neighbours, owners, low, own, high, velocity):
    return pl.pallas_call(
        contact_kernel,
        out_shape=jax.ShapeDtypeStruct((BRICKS * CAP * LATE, PB), F32),
        in_specs=[smem(), smem(), vmem(), vmem(), vmem(), vmem()],
        out_specs=vmem(),
        scratch_shapes=[
            pltpu.VMEM((4, PB, PB), BF16),
            pltpu.VMEM((NB * FEAT, PB), F32),
            pltpu.VMEM((3 * NB // 4, PB, PB), BF16),
            pltpu.VMEM((NB, FEAT, 2 * PB), BF16),
            pltpu.VMEM((NB * FEAT, PB), F32),
            pltpu.VMEM((3 * NB, FEAT, PB), BF16),
            pltpu.VMEM((NB, FEAT, 2 * PB), F32),
            pltpu.VMEM((LATE, NB, PB), F32),
            pltpu.SMEM((BRICKS,), jnp.int32),
        ],
        compiler_params=pltpu.CompilerParams(vmem_limit_bytes=40 * 1024 * 1024),
        cost_estimate=pl.CostEstimate(flops=20_000_000_000, bytes_accessed=8_000_000, transcendentals=9_437_184),
        name="contact_payload",
    )(neighbours, owners, low, own, high, velocity)


def tap(distance):
    weights = kernel_weights()
    value = jnp.zeros(distance.shape, F32)
    for t in range(RAD + 1):
        value = jnp.where(jnp.abs(distance) == t, weights[RAD + t], value)
    return value


def split2(value):
    high = value.astype(BF16)
    return high, (value - high.astype(F32)).astype(BF16)


def deposit_kernel(even, early, late, arrived, tile, send_a, send_b, grid):
    grid[...] = jnp.zeros_like(grid)
    group = 2
    width = group * CAP * PB

    def chunk(c, carry):
        slots = [(c * group + s, q) for s in range(group) for q in range(CAP)]
        cells = jnp.concatenate(
            [early[s, EARLY * q + 4 : EARLY * q + 5, :] for s, q in slots], axis=1
        ).astype(jnp.int32)
        reach = jnp.concatenate([early[s, EARLY * q + 3 : EARLY * q + 4, :] for s, q in slots], axis=1)
        mass = 8.0 * reach * reach * reach
        rest = jnp.concatenate([late[s, LATE * q + 3 : LATE * q + 12, :] for s, q in slots], axis=1)
        fields = jnp.concatenate([rest[:6], mass, rest[6:9]], axis=0)
        across = lax.broadcasted_iota(jnp.int32, (CZ * CY, width), 0) == cells // CX
        along = jnp.where(
            lax.broadcasted_iota(jnp.int32, (CX, width), 0) == cells % CX, 1.0, 0.0
        ).astype(BF16)
        weighted = jnp.concatenate(
            [jnp.where(across, fields[f : f + 1], 0.0).astype(BF16) for f in range(FIELDS)], axis=0
        )
        grid[...] += lax.dot_general(
            weighted, along, (((1,), (1,)), ((), ())), preferred_element_type=F32
        )
        return carry

    lax.fori_loop(0, BRICKS // group, chunk, 0)

    def arrive(s, carry):
        for q in range(CAP):
            velocity = late[s, LATE * q : LATE * q + 3, :]
            arrived[s * CAP + q, 3:6, :] = velocity
            arrived[s * CAP + q, 0:3, :] = early[s, EARLY * q : EARLY * q + 3, :] + TIMESTEP * velocity
        return carry

    lax.fori_loop(0, BRICKS, arrive, 0)
    rows = lax.broadcasted_iota(jnp.int32, (CX, CX), 0)
    band_high, band_low = split2(tap(rows - lax.broadcasted_iota(jnp.int32, (CX, CX), 1)))

    def smooth(f, carry):
        high, low = split2(grid[pl.ds(pl.multiple_of(f * CZ * CY, CZ * CY), CZ * CY), :])
        value = jnp.dot(jnp.concatenate([high, low], axis=0), band_high, preferred_element_type=F32)
        tile[f] = value[: CZ * CY] + value[CZ * CY :] + jnp.dot(high, band_low, preferred_element_type=F32)
        return carry

    lax.fori_loop(0, FIELDS, smooth, 0)

    def border(target, first):
        for f in range(FIELDS):
            for z in range(CZ):
                target[f, z * RAD : (z + 1) * RAD, :] = tile[f, z * CY + first : z * CY + first + RAD, :]

    @pl.when(even[0] == 1)
    def _():
        border(send_a, CY - RAD)
        border(send_b, 0)

    @pl.when(even[0] == 0)
    def _():
        border(send_a, 0)
        border(send_b, CY - RAD)


def deposit(even, early, late):
    side = jax.ShapeDtypeStruct((FIELDS, CZ * RAD, CX), F32)
    return pl.pallas_call(
        deposit_kernel,
        out_shape=(
            jax.ShapeDtypeStruct((BRICKS * CAP, 6, PB), F32),
            jax.ShapeDtypeStruct((FIELDS, CZ * CY, CX), F32),
            side,
            side,
        ),
        in_specs=[smem(), vmem(), vmem()],
        out_specs=(vmem(), vmem(), vmem(), vmem()),
        scratch_shapes=[pltpu.VMEM((FIELDS * CZ * CY, CX), F32)],
        compiler_params=pltpu.CompilerParams(vmem_limit_bytes=40 * 1024 * 1024),
        cost_estimate=pl.CostEstimate(flops=12_000_000_000, bytes_accessed=8_000_000, transcendentals=0),
        name="deposit",
    )(even, early, late)


def halo_weights(even, along_rows):
    def line(value):
        return value % CY if along_rows else value // CY

    def other(value):
        return value // CY if along_rows else value % CY

    def side_line(value):
        return value % RAD if along_rows else value // CY

    def side_other(value):
        return value // RAD if along_rows else value % CY

    def part(count, place, same):
        out = lax.broadcasted_iota(jnp.int32, (CZ * CY, count), 0)
        source = lax.broadcasted_iota(jnp.int32, (CZ * CY, count), 1)
        return jnp.where(other(out) == same(source), tap(place(source) - line(out)), 0.0)

    above = RAD * CY
    return jnp.concatenate(
        [
            part(CZ * CY, line, other),
            part(above, lambda v: side_line(v) + jnp.where(even == 1, CY, -RAD), side_other),
            part(above, lambda v: side_line(v) + jnp.where(even == 1, -RAD, CY), side_other),
        ],
        axis=1,
    )


def smooth_all(weights, tile, side_a, side_b, out):
    weight_high, weight_low = split2(weights)
    both = jnp.concatenate([weight_high, weight_low], axis=0)
    rows = CZ * CY

    def smooth(f, carry):
        value = jnp.concatenate([tile[f], side_a[f], side_b[f]], axis=0)
        high, low = split2(value)
        part = jnp.dot(both, high, preferred_element_type=F32)
        result = part[:rows] + part[rows:] + jnp.dot(weight_high, low, preferred_element_type=F32)
        out[f] = result.reshape(out.shape[1:])
        return carry

    lax.fori_loop(0, FIELDS, smooth, 0, unroll=2)


def smooth_rows_kernel(even, slab_even, tile, side_a, side_b, out, send_a, send_b):
    smooth_all(halo_weights(even[0], True), tile, side_a, side_b, out)
    rows = RAD * CY
    top = CZ * CY - rows

    @pl.when(slab_even[0] == 1)
    def _():
        send_a[...] = out[:, top:, :]
        send_b[...] = out[:, :rows, :]

    @pl.when(slab_even[0] == 0)
    def _():
        send_a[...] = out[:, :rows, :]
        send_b[...] = out[:, top:, :]


def smooth_rows(even, slab_even, tile, side_a, side_b):
    side = jax.ShapeDtypeStruct((FIELDS, CY * RAD, CX), F32)
    return pl.pallas_call(
        smooth_rows_kernel,
        out_shape=(jax.ShapeDtypeStruct((FIELDS, CZ * CY, CX), F32), side, side),
        in_specs=[smem(), smem(), vmem(), vmem(), vmem()],
        out_specs=(vmem(), vmem(), vmem()),
        compiler_params=pltpu.CompilerParams(vmem_limit_bytes=40 * 1024 * 1024),
        name="smooth_rows",
    )(even, slab_even, tile, side_a, side_b)


def smooth_layers_kernel(slab_even, tile, side_a, side_b, out):
    smooth_all(halo_weights(slab_even[0], False), tile, side_a, side_b, out)


def smooth_layers(slab_even, tile, side_a, side_b):
    return pl.pallas_call(
        smooth_layers_kernel,
        out_shape=jax.ShapeDtypeStruct((FIELDS, CZ, CY, CX), F32),
        in_specs=[smem(), vmem(), vmem(), vmem()],
        out_specs=vmem(),
        compiler_params=pltpu.CompilerParams(vmem_limit_bytes=40 * 1024 * 1024),
        name="smooth_layers",
    )(slab_even, tile, side_a, side_b)


def swap_near(value, axis, count):
    return lax.ppermute(value, axis, [(i, i ^ 1) for i in range(count)])


def swap_far(value, axis, count):
    return lax.ppermute(value, axis, [(i, i + 1 if i % 2 else i - 1) for i in range(1, count - 1)])


def body(positions, velocities, radius, owners, neighbours, cell_index):
    brick, slab = lax.axis_index("brick"), lax.axis_index("slab")
    even = (1 - brick % 2).astype(jnp.int32)
    slab_even = (1 - slab % 2).astype(jnp.int32).reshape(1)
    place = jnp.transpose(positions, (1, 0, 2))
    velocity = jnp.transpose(velocities, (1, 0, 2))
    packed = jnp.concatenate([place, radius[None]], axis=0)
    early = early_payload(owners, place, radius, cell_index)
    early = lax.all_to_all(
        early.reshape(BRICKS, CAP * EARLY, PB), "brick", split_axis=0, concat_axis=0, tiled=True
    )
    near = swap_near(packed, "brick", BRICKS)
    far = swap_far(packed, "brick", BRICKS)
    swapped = jnp.where(neighbours < NB, neighbours + 2 * NB, jnp.where(neighbours >= 2 * NB, neighbours - 2 * NB, neighbours))
    places = jnp.where(even == 1, swapped, neighbours)
    late = contact_payload(places, owners, near, packed, far, velocity)
    late = lax.all_to_all(
        late.reshape(BRICKS, CAP * LATE, PB), "brick", split_axis=0, concat_axis=0, tiled=True
    )
    even = even.reshape(1)
    arrived, tile, send_a, send_b = deposit(even, early, late)
    side_a = swap_near(send_a, "brick", BRICKS)
    side_b = swap_far(send_b, "brick", BRICKS)
    rows, send_a, send_b = smooth_rows(even, slab_even, tile, side_a, side_b)
    side_a = swap_near(send_a, "slab", SLABS)
    side_b = swap_far(send_b, "slab", SLABS)
    return arrived, smooth_layers(slab_even, rows, side_a, side_b)


def solution(mesh):
    return jax.shard_map(
        body,
        mesh=mesh,
        in_specs=(
            P(("slab", "brick"), None, None),
            P(("slab", "brick"), None, None),
            P(("slab", "brick"), None),
            P(("slab", "brick")),
            P(("slab", "brick"), None),
            P(("slab", "brick"), None),
        ),
        out_specs=(P(("slab", "brick"), None, None), P(None, "slab", "brick", None)),
        check_vma=False,
    )
```

time: 267 us -> 145 us (0.54)
  other arithmetic: 133 us -> 0.98 us
  Pallas kernels: 0 us -> 59 us
  waiting for transfers between devices: 63.8 us -> 27.4 us
  blocking collectives: 0 us -> 33.9 us
  matrix products: 18.3 us -> 0 us
  starting transfers between devices: 34.1 us -> 21.1 us
  local copies, waits for them, and re-layouts: 12.8 us -> 1.29 us
  loops' own time: 2.94 us -> 0 us
    reduce_sum x50 -> x0, other arithmetic: 119 us -> none  [the longest x16 79.1 us: pair_terms(): jnp.sum(fabric_scale * offset[:, :, a] * offset[:, :, a], axis=(1, 3))]
    pallas_call x0 -> x5, Pallas kernels: none -> 59 us  [the longest x1 33.8 us: contact_payload(): pl.pallas_call(contact_kernel, out_shape=jax.ShapeDtypeStruct((BRICKS * C...]
    all_to_all x2 -> x1, waiting for transfers between devices: 36.5 us -> 0.01 us  [body(): lax.all_to_all(early.reshape(BRICKS, CAP * EARLY, PB), 'brick', split_axi...]
    all_to_all x0 -> x1, blocking collectives: none -> 33.9 us  [body(): lax.all_to_all(late.reshape(BRICKS, CAP * LATE, PB), 'brick', split_axis=...]
    dot_general x16 -> x0, matrix products: 18.3 us -> none  [accumulate(): jnp.einsum('frgp,gpx->frx', weighted, along, preferred_element_type=jnp.f...]
    add x5 -> x0, other arithmetic: 6.73 us -> none  [the longest x3 5.97 us: blur(): result + weights[t] * lax.slice_in_dim(field_data, t, t + extent, axis=ax...]
    ppermute x6, starting transfers between devices: 17.1 us -> 10.5 us  [the longest x3 8.96 us: swap_far(): lax.ppermute(value, axis, [(i, i + 1 if i % 2 else i - 1) for i in range(...]
    all_to_all x2 -> x1, starting transfers between devices: 16.9 us -> 10.6 us  [body(): lax.all_to_all(early.reshape(BRICKS, CAP * EARLY, PB), 'brick', split_axi...]
  transfers between devices with their start and end apart: 8 -> 7, of which waited for: 6 -> 2; matrix products, arithmetic and copies ran while one was open for 3% -> 1% of each run, Pallas kernels for 0% -> 25%
where the time goes in v1:
time: 145 us; the launch traced here: 144 us
  Pallas kernels  59 us (41%)
  blocking collectives  33.9 us (23%)
  waiting for transfers between devices  27.4 us (19%)
  starting transfers between devices  21.1 us (15%)
    all_to_all x1, blocking collectives, body(): lax.all_to_all(late.reshape(BRICKS, CAP * LATE, PB), 'brick', split_axis=...  33.9 us
    pallas_call x1, Pallas kernels, contact_payload(): pl.pallas_call(contact_kernel, out_shape=jax.ShapeDtypeStruct((BRICKS * C...  33.8 us
    ppermute x3, waiting for transfers between devices, swap_near(): return lax.ppermute(value, axis, [(i, i ^ 1) for i in range(count)])  19.2 us
    pallas_call x1, Pallas kernels, deposit(): pl.pallas_call(deposit_kernel, out_shape=(jax.ShapeDtypeStruct((BRICKS *...  18.7 us
    all_to_all x1, starting transfers between devices, body(): lax.all_to_all(early.reshape(BRICKS, CAP * EARLY, PB), 'brick', split_axi...  10.6 us
    ppermute x3, starting transfers between devices, swap_far(): lax.ppermute(value, axis, [(i, i + 1 if i % 2 else i - 1) for i in range(...  8.96 us
    ppermute x3, waiting for transfers between devices, swap_far(): lax.ppermute(value, axis, [(i, i + 1 if i % 2 else i - 1) for i in range(...  8.2 us
  transfers between devices with their start and end apart: 7, of which 2 were waited for; matrix products, arithmetic and copies ran while one was open for 1% of the time, Pallas kernels for 25%

profile of v1, /device:TPU:37, one launch (start us, length us, event | category | flops | bytes accessed | tf_op | source)
XLA Modules:
  0.0 144.5 jit_solution(2227797637320200188)
XLA Ops:
  0.6 0.0 copy-start
  0.6 0.0 copy-start.2
  0.7 0.0 copy-start.1
  0.7 1.0 pad_maximum_fusion.own
  1.6 4.1 %collective-permute-start.1 = (f32[4,64,128]{2,1,0:T(8,128)S(1)}, f32[4,64,128]{2,1,0:T(8,128)S(1)}, u32[]{:S(2)}, u32[]{:S(2)}) collective-permute-start(f32[4,64,128]{2,1,0:T(8,128)S(1)} %pad_maximum_fusion.own), channel_id=1, source_target_pairs={{1,2},{2,1},{3,4},{4,3},{5,6},{6,5},{7,8},{8,7},{9,10},{10,9},{11,... | collective-permute-start | bytes 393224 | tf_op jit(solution)/shard_map/ppermute | solution.py:420
  5.7 0.1 collective-permute-start
  5.8 2.6 %early_payload.1 = f32[768,128]{1,0:T(8,128)} custom-call(s32[64]{0:T(128)} %owners.3, f32[3,64,128]{2,1,0:T(8,128)} %bitcast.11, f32[64,128]{1,0:T(8,128)} %radius.1, s32[64,128]{1,0:T(8,128)} %cells.1), custom_call_target="tpu_custom_call" | custom-call | tf_op jit(solution)/shard_map/early_payload/pallas_call | solution.py:87
  8.4 10.6 %all-to-all-start = ((f32[32,24,128]{2,1,0:T(8,128)}), f32[32,24,128]{2,1,0:T(8,128)S(1)}, u32[]{:S(2)}, u32[]{:S(2)}) async-start(f32[32,24,128]{2,1,0:T(8,128)} %bitcast.9), calls=%async_computation | async-start | bytes 786432 | tf_op jit(solution)/shard_map/all_to_all | solution.py:431
  19.1 0.0 copy-done.2
  19.1 0.1 copy.21
  19.2 0.1 copy.19
  19.3 0.1 copy.22
  19.4 0.1 copy.20
  19.5 0.1 copy.23
  19.6 0.0 collective-permute-done.1.high
  19.6 0.0 collective-permute-done.low
  19.6 0.0 copy-done
  19.6 0.0 copy-done.1
  19.6 33.8 %contact_payload.1 = f32[1536,128]{1,0:T(8,128)S(1)} custom-call(s32[64,8]{1,0:T(8,128)S(1)} %select_select_fusion.neighbours, s32[64]{0:T(128)S(1)} %copy-done, f32[4,64,128]{2,1,0:T(8,128)S(1)} %collective-permute-done.low, f32[4,64,128]{2,1,0:T(8,128)S(1)} %pad_maximum_fusion.own, f32[4,64,128]{2,1,0:T(8,128)S(1)} %collective-permute-done.1.high, ...), custom_call_target="tpu_custom_call" | custom-call | flops 20000000000 | bytes 8000000 | tf_op jit(solution)/shard_map/contact_payload/pallas_call | solution.py:210
  53.4 0.0 all-to-all-done.early
  53.4 33.9 %all_to_all.10.late = f32[32,48,128]{2,1,0:T(8,128)S(1)} all-to-all(f32[32,48,128]{2,1,0:T(8,128)S(1)} %bitcast.7), channel_id=1, replica_groups=mesh['slab'=8,'brick'=32] {'brick'}, dimensions={0} | all-to-all | bytes 1572864 | tf_op jit(solution)/shard_map/all_to_all | solution.py:439
  87.3 18.7 %deposit.1 = (f32[128,6,128]{2,1,0:T(8,128)S(1)}, f32[10,64,512]{2,1,0:T(8,128)S(1)}, f32[10,24,512]{2,1,0:T(8,128)}, f32[10,24,512]{2,1,0:T(8,128)S(1)}) custom-call(s32[1]{0:T(128)} %bitcast.even, f32[32,24,128]{2,1,0:T(8,128)S(1)} %all-to-all-done.early, f32[32,48,128]{2,1,0:T(8,128)S(1)} %all_to_all.10.late), custom_call_target="tpu_custom_call" | custom-call | flops 12000000000 | bytes 8000000 | tf_op jit(solution)/shard_map/deposit/pallas_call | solution.py:310
  106.0 1.0 collective-permute-start.2
  107.0 1.9 %collective-permute-start.3 = (f32[10,24,512]{2,1,0:T(8,128)S(1)}, f32[10,24,512]{2,1,0:T(8,128)S(1)}, u32[]{:S(2)}, u32[]{:S(2)}) collective-permute-start(f32[10,24,512]{2,1,0:T(8,128)S(1)} %get-tuple-element.12), channel_id=1, source_target_pairs={{1,2},{2,1},{3,4},{4,3},{5,6},{6,5},{7,8},{8,7},{9,10},{10,9},{11,... | collective-permute-start | bytes 1474568 | tf_op jit(solution)/shard_map/ppermute | solution.py:420
  108.9 0.0 collective-permute-done.2.side_a
  108.9 8.2 %collective-permute-done.3.side_b = f32[10,24,512]{2,1,0:T(8,128)S(1)} collective-permute-done((f32[10,24,512]{2,1,0:T(8,128)S(1)}, f32[10,24,512]{2,1,0:T(8,128)S(1)}, u32[]{:S(2)}, u32[]{:S(2)}) %collective-permute-start.3) | collective-permute-done | bytes 491552 | tf_op jit(solution)/shard_map/ppermute | solution.py:420
  117.1 1.4 smooth_rows.1
  118.6 0.5 collective-permute-start.4
  119.1 2.9 %collective-permute-start.5 = (f32[10,24,512]{2,1,0:T(8,128)S(1)}, f32[10,24,512]{2,1,0:T(8,128)S(1)}, u32[]{:S(2)}, u32[]{:S(2)}) collective-permute-start(f32[10,24,512]{2,1,0:T(8,128)S(1)} %get-tuple-element.15), channel_id=1, source_target_pairs={{32,64},{64,32},{96,128},{128,96},{160,192},{192,160},{33,65},{65,... | collective-permute-start | bytes 1474568 | tf_op jit(solution)/shard_map/ppermute | solution.py:420
  122.0 0.8 copy.25
  122.8 19.2 %collective-permute-done.4.side_a = f32[10,24,512]{2,1,0:T(8,128)S(1)} collective-permute-done((f32[10,24,512]{2,1,0:T(8,128)S(1)}, f32[10,24,512]{2,1,0:T(8,128)S(1)}, u32[]{:S(2)}, u32[]{:S(2)}) %collective-permute-start.4) | collective-permute-done | bytes 491552 | tf_op jit(solution)/shard_map/ppermute | solution.py:416
  142.0 0.0 collective-permute-done.5.side_b
  142.0 2.4 %smooth_layers.1 = f32[10,8,8,512]{3,2,1,0:T(8,128)} custom-call(s32[1]{0:T(128)} %bitcast.6.slab_even, f32[10,64,512]{2,1,0:T(8,128)S(1)} %get-tuple-element.13.tile, f32[10,24,512]{2,1,0:T(8,128)S(1)} %collective-permute-done.4.side_a, f32[10,24,512]{2,1,0:T(8,128)S(1)} %collective-permute-done.5.side_b), custom_call_target="tpu_custom_call" | custom-call | tf_op jit(solution)/shard_map/smooth_layers/pallas_call | solution.py:405
  (3 shorter events, 0.0 us)
Async XLA Ops:
  0.6 19.0 %copy-start = (s32[64]{0:T(128)S(1)}, s32[64]{0:T(128)}, u32[]{:S(2)}) copy-start(s32[64]{0:T(128)} %owners.3) | copy-start | bytes 772
  0.6 18.4 %copy-start.2 = (s32[64,8]{0,1:T(8,128)S(1)}, s32[64,8]{0,1:T(8,128)}, u32[]{:S(2)}) copy-start(s32[64,8]{0,1:T(8,128)} %param.10) | copy-start | bytes 6148
  0.7 18.9 %copy-start.1 = (f32[64,3,128]{2,0,1:T(8,128)S(1)}, f32[64,3,128]{2,0,1:T(8,128)}, u32[]{:S(2)}) copy-start(f32[64,3,128]{2,0,1:T(8,128)} %param.7) | copy-start | bytes 294916
  1.6 17.9 %collective-permute-start.1 = (f32[4,64,128]{2,1,0:T(8,128)S(1)}, f32[4,64,128]{2,1,0:T(8,128)S(1)}, u32[]{:S(2)}, u32[]{:S(2)}) collective-permute-start(f32[4,64,128]{2,1,0:T(8,128)S(1)} %pad_maximum_fusion.own), channel_id=1, source_target_pairs={{1,2},{2,1},{3,4},{4,3},{5,6},{6,5},{7,8},{8,7},{9,10},{10,9},{11,... | collective-permute-start | bytes 393224 | tf_op jit(solution)/shard_map/ppermute | solution.py:420
  5.7 13.8 %collective-permute-start = (f32[4,64,128]{2,1,0:T(8,128)S(1)}, f32[4,64,128]{2,1,0:T(8,128)S(1)}, u32[]{:S(2)}, u32[]{:S(2)}) collective-permute-start(f32[4,64,128]{2,1,0:T(8,128)S(1)} %pad_maximum_fusion.own), channel_id=1, source_target_pairs={{0,1},{1,0},{2,3},{3,2},{4,5},{5,4},{6,7},{7,6},{8,9},{9,8},{10,11... | collective-permute-start | bytes 393224 | tf_op jit(solution)/shard_map/ppermute | solution.py:416
  8.4 44.9 %all-to-all-start = ((f32[32,24,128]{2,1,0:T(8,128)}), f32[32,24,128]{2,1,0:T(8,128)S(1)}, u32[]{:S(2)}, u32[]{:S(2)}) async-start(f32[32,24,128]{2,1,0:T(8,128)} %bitcast.9), calls=%async_computation | async-start | bytes 786432 | tf_op jit(solution)/shard_map/all_to_all | solution.py:431
  106.0 2.9 %collective-permute-start.2 = (f32[10,24,512]{2,1,0:T(8,128)}, f32[10,24,512]{2,1,0:T(8,128)S(1)}, u32[]{:S(2)}, u32[]{:S(2)}) collective-permute-start(f32[10,24,512]{2,1,0:T(8,128)} %get-tuple-element.11), channel_id=1, source_target_pairs={{0,1},{1,0},{2,3},{3,2},{4,5},{5,4},{6,7},{7,6},{8,9},{9,8},{10,11... | collective-permute-start | bytes 1474568 | tf_op jit(solution)/shard_map/ppermute | solution.py:416
  107.0 10.1 %collective-permute-start.3 = (f32[10,24,512]{2,1,0:T(8,128)S(1)}, f32[10,24,512]{2,1,0:T(8,128)S(1)}, u32[]{:S(2)}, u32[]{:S(2)}) collective-permute-start(f32[10,24,512]{2,1,0:T(8,128)S(1)} %get-tuple-element.12), channel_id=1, source_target_pairs={{1,2},{2,1},{3,4},{4,3},{5,6},{6,5},{7,8},{8,7},{9,10},{10,9},{11,... | collective-permute-start | bytes 1474568 | tf_op jit(solution)/shard_map/ppermute | solution.py:420
  118.6 23.5 %collective-permute-start.4 = (f32[10,24,512]{2,1,0:T(8,128)S(1)}, f32[10,24,512]{2,1,0:T(8,128)S(1)}, u32[]{:S(2)}, u32[]{:S(2)}) collective-permute-start(f32[10,24,512]{2,1,0:T(8,128)S(1)} %get-tuple-element.14), channel_id=1, source_target_pairs={{0,32},{32,0},{64,96},{96,64},{128,160},{160,128},{192,224},{224,1... | collective-permute-start | bytes 1474568 | tf_op jit(solution)/shard_map/ppermute | solution.py:416
  119.1 23.0 %collective-permute-start.5 = (f32[10,24,512]{2,1,0:T(8,128)S(1)}, f32[10,24,512]{2,1,0:T(8,128)S(1)}, u32[]{:S(2)}, u32[]{:S(2)}) collective-permute-start(f32[10,24,512]{2,1,0:T(8,128)S(1)} %get-tuple-element.15), channel_id=1, source_target_pairs={{32,64},{64,32},{96,128},{128,96},{160,192},{192,160},{33,65},{65,... | collective-permute-start | bytes 1474568 | tf_op jit(solution)/shard_map/ppermute | solution.py:420
